TPU v7x, 512 devices: a whole 4x8x8 slice. The times are simulated.
512 devices in a mesh: wide: 64 (over x, y, core), narrow: 8 (over z).
Axes of the slice: x: 4, y: 8, z: 8, core: 2. Of those that a mesh axis runs over, the one named last changes fastest.
Arguments:
- node_coords: float32 [3, 64, 8, 9, 256], P(None, 'wide', 'narrow'), may hold values from -192 to 192, as said below
- solution: float32 [2, 64, 8, 9, 256], P(None, 'wide', 'narrow'), may hold values from -6 to 6
- residual: float32 [2, 64, 8, 9, 256], P(None, 'wide', 'narrow'), may hold values from -6 to 6
- direction: float32 [2, 64, 8, 9, 256], P(None, 'wide', 'narrow'), may hold values from -6 to 6
- tile_pairs: int32 [64, 8, 2, 61], P('wide', 'narrow'), may hold values from 0 to 80, as said below
- tile_counts: int32 [64, 8], P('wide', 'narrow'), may hold values from 1 to 61
Outputs:
- new_solution: float32 [2, 64, 8, 9, 256], P(None, 'wide', 'narrow')
- new_residual: float32 [2, 64, 8, 9, 256], P(None, 'wide', 'narrow')
- new_direction: float32 [2, 64, 8, 9, 256], P(None, 'wide', 'narrow')
Inputs may be any that keep to these rules, and one draw needn't show every extreme that they name: `tile_pairs`: neighbourhood indices lie in 0 to 80. In live slots every unordered pair of blocks appears at most once over all devices, one of its two blocks is owned by the device that holds the slot, the two blocks lie on devices at most one step apart along each direction (wide taken around its loop), and no live index points past the bounded ends of the narrow direction. Slots past a device's count hold arbitrary indices. `node_coords`: distinct nodes; the operator M built from the live tiles is symmetric positive definite.
All inputs are finite; a program needn't handle non-finite values.
Results may differ from a plain program's by a relative error of at most 0.00095.
Values sent between devices are 32-bit elements; how exact they have to be, the bound alone decides.
A program may use at most 64 MiB of HBM per device.

v0:
```python
import functools

import jax
import jax.numpy as jnp
from jax import lax
from jax.experimental import pallas as pl
from jax.experimental.pallas import tpu as pltpu
from jax.sharding import PartitionSpec as P

ITERS = 3
RADIUS = 0.9
MESH = pl.DeviceIdType.MESH
F32 = jnp.float32
BF16 = jnp.bfloat16

BLOCKS = 9
NODES = 256
SLOTS = 61
ROWS = 40
TABLE = 368
GROUP = 3
CHUNK = 16

PHI_SLOPE = 4.0 / RADIUS**5
PHI_CONST = 1.0 / RADIUS**4


def dot_bf16(left, right, transposed):
    dims = (((1,), (1 if transposed else 0,)), ((), ()))
    return lax.dot_general(left, right, dims, preferred_element_type=F32)


def split(value):
    high = value.astype(BF16)
    return high, (value - high.astype(F32)).astype(BF16)


def stage_peers(wide, narrow, stages):
    peers = []
    for axis, places in stages:
        here = wide if axis == "wide" else narrow
        rank, size = 0, 1
        for stride, count in places:
            rank = rank * count + here // stride % count
            size *= count
        group = []
        for step in range(1, size):
            other = (rank + step) % size
            position = here
            left = other
            for stride, count in reversed(places):
                position = position + (left % count - here // stride % count) * stride
                left = left // count
            group.append((position, narrow) if axis == "wide" else (wide, position))
        peers.append(group)
    return peers


def general_body(
    sizes,
    stages,
    coord_ref,
    sol_ref,
    res_ref,
    dir_ref,
    pairs_hbm_ref,
    count_ref,
    new_sol_ref,
    new_res_ref,
    new_dir_ref,
    near0,
    nearq,
    part,
    got,
    khi_even,
    klo_even,
    khi_odd,
    klo_odd,
    thi_even,
    tlo_even,
    thi_odd,
    tlo_odd,
    stage_even,
    stage_odd,
    pieces,
    slot_out,
    onehot,
    basis,
    sums,
    sum_in,
    raw,
    sol_rows,
    pairs_ref,
    pairs_vec_ref,
    cols,
    load_sems,
    near_send,
    near_recv,
    q_send,
    q_recv,
    fold_send,
    fold_recv,
    sum_send,
    sum_recv,
):
    wide_size, narrow_size = sizes
    wide = lax.axis_index("wide")
    narrow = lax.axis_index("narrow")
    neighbours = []
    for d in range(9):
        if d != 4:
            to_wide = (wide + (d // 3 - 1) + wide_size) % wide_size
            to_narrow = (narrow + (d % 3 - 1) + narrow_size) % narrow_size
            neighbours.append((d, (to_wide, to_narrow)))
    peers = stage_peers(wide, narrow, stages)

    loads = [
        pltpu.make_async_copy(source, landing, load_sems.at[at])
        for at, (source, landing) in enumerate(
            (
                (dir_ref, raw.at[pl.ds(0, 2 * BLOCKS)]),
                (res_ref, raw.at[pl.ds(2 * BLOCKS, 2 * BLOCKS)]),
                (coord_ref, raw.at[pl.ds(4 * BLOCKS, 3 * BLOCKS)]),
                (pairs_hbm_ref, pairs_ref),
                (pairs_hbm_ref, pairs_vec_ref),
                (sol_ref, sol_rows),
            )
        )
    ]
    for load in loads:
        load.start()

    barrier = pltpu.get_barrier_semaphore()
    targets = [device for _, device in neighbours] + [device for group in peers for device in group]
    for device in targets:
        pl.semaphore_signal(barrier, inc=1, device_id=device, device_id_type=MESH)

    for load in loads:
        load.wait()
    for k in range(BLOCKS):
        own = 4 * BLOCKS + k
        for c in range(7):
            near0[own, c : c + 1, :] = raw[c * BLOCKS + k]
        near0[own, 7:8, :] = jnp.zeros((1, NODES), F32)

    pl.semaphore_wait(barrier, len(targets))

    pending = []

    def exchange(source, landing, send_sem, recv_sem):
        copies = []
        for at, (d, device) in enumerate(neighbours):
            copy = pltpu.make_async_remote_copy(
                src_ref=source(d),
                dst_ref=landing(8 - d, 7 - at),
                send_sem=send_sem.at[at],
                recv_sem=recv_sem.at[7 - at],
                device_id=device,
                device_id_type=MESH,
            )
            copy.start()
            copies.append(copy)
        pending.extend(copies)

        def wait(at):
            pltpu.make_async_remote_copy(
                src_ref=source(4),
                dst_ref=landing(at + at // 4, at),
                send_sem=send_sem.at[at],
                recv_sem=recv_sem.at[at],
                device_id=neighbours[0][1],
                device_id_type=MESH,
            ).wait_recv()

        return wait

    arrive = exchange(
        lambda d: near0.at[pl.ds(4 * BLOCKS, BLOCKS)],
        lambda d, at: near0.at[pl.ds(d * BLOCKS, BLOCKS)],
        near_send,
        near_recv,
    )

    slot_of = lax.broadcasted_iota(jnp.int32, (64, 512), 0)
    lane_slot = lax.broadcasted_iota(jnp.int32, (64, 512), 1) // 8
    spread = jnp.where(slot_of == lane_slot, 1.0, 0.0).astype(BF16)
    left_id = pairs_vec_ref[0:1, :]
    right_id = pairs_vec_ref[1:2, :]
    live = lax.broadcasted_iota(jnp.int32, (1, SLOTS), 1) < count_ref[0:1, 0:1]
    toward_left = jnp.where(live, left_id, 255)
    toward_right = jnp.where(live & (left_id != right_id), right_id, 255)
    ids = jnp.concatenate([toward_right, toward_left] + [toward_left] * 6, axis=0).astype(F32)
    ids = jnp.concatenate([ids, jnp.full((8, 64 - SLOTS), 255.0, F32)], axis=1)
    wanted = dot_bf16(ids.astype(BF16), spread, False)
    lane = lax.broadcasted_iota(jnp.int32, (8, 512), 1)
    target = jnp.where(lane % 8 < 4, wanted[0:1, :], wanted[1:2, :]).astype(jnp.int32)
    for first in range(0, TABLE, CHUNK):
        row = lax.broadcasted_iota(jnp.int32, (CHUNK, 512), 0) + first
        place = row % ROWS
        block = jnp.where(place < 4 * BLOCKS, row // ROWS * BLOCKS + place // 4, 200)
        match = (block == target[0:1, :]) & (
            row % 4 == lax.broadcasted_iota(jnp.int32, (CHUNK, 512), 1) % 4
        )
        onehot[pl.ds(first, CHUNK), :] = jnp.where(match, 1.0, 0.0).astype(BF16)

    slot_out[pl.ds(8 * SLOTS, 512 - 8 * SLOTS), :] = jnp.zeros((512 - 8 * SLOTS, NODES), F32)
    half = lax.broadcasted_iota(jnp.int32, (8, NODES), 0) < 4

    def put_pieces(j, rows_at, value):
        high = value.astype(BF16).astype(F32)
        low = value - high
        if rows_at == 0:
            rows = jnp.where(half, high, pltpu.roll(low, 4, 0))
        else:
            rows = jnp.where(half, pltpu.roll(high, 4, 0), low)
        pieces[j] = jnp.concatenate([rows, rows], axis=0).astype(BF16)

    for h in range(2):
        for k in range(BLOCKS):
            basis[0, h, 4 * k : 4 * k + 4, :] = near0[4 * BLOCKS + k, 0:4, 128 * h : 128 * h + 128]
        basis[0, h, 4 * BLOCKS : ROWS, :] = jnp.zeros((ROWS - 4 * BLOCKS, 128), F32)

    def prepare(d):
        for k in range(BLOCKS):
            j = d * BLOCKS + k
            value = near0[j]
            put_pieces(j, 0, value)
            cols[j] = jnp.transpose(value)

    def prepare_next(at, carry):
        arrive(at)
        prepare(at + at // 4)
        return carry

    prepare(4)
    lax.fori_loop(0, 8, prepare_next, 0)

    def evaluate(s, refs, stage, at):
        high_ref, low_ref, high_turned, low_turned = refs
        left = cols.at[pairs_ref[0, s]]
        right = near0[pairs_ref[1, s]]
        rights = [jnp.broadcast_to(right[4 + axis : 5 + axis, :], (CHUNK, NODES)) for axis in range(3)]
        for first in range(0, NODES, CHUNK):
            column = left[first : first + CHUNK, :]
            squared = None
            for axis in range(3):
                offset = column[:, 4 + axis : 5 + axis] - rights[axis]
                squared = offset * offset if squared is None else squared + offset * offset
            squared = jnp.minimum(squared, RADIUS * RADIUS)
            distance = squared * lax.rsqrt(jnp.maximum(squared, 1e-36))
            rest = RADIUS - distance
            rest = rest * rest
            rest = rest * rest
            value = rest * (PHI_SLOPE * distance + PHI_CONST)
            high, low = split(value)
            high_ref[at, first : first + CHUNK, :] = high
            low_ref[at, first : first + CHUNK, :] = low
            stage[first : first + CHUNK, :] = value
        for first in range(0, NODES, 128):
            high, low = split(jnp.transpose(stage[first : first + 128, :]))
            high_turned[at, :, first : first + 128] = high
            low_turned[at, :, first : first + 128] = low

    def product(s, refs, at):
        high_ref, low_ref, high_turned, low_turned = refs
        left = pieces[pairs_ref[0, s]]
        right = pieces[pairs_ref[1, s]]
        to_right = dot_bf16(left, high_ref[at], False) + dot_bf16(left, low_ref[at], False)
        to_left = dot_bf16(right, high_turned[at], False) + dot_bf16(right, low_turned[at], False)
        to_right = to_right[0:8]
        to_left = to_left[0:8]
        to_right = to_right + pltpu.roll(to_right, 4, 0)
        to_left = to_left + pltpu.roll(to_left, 4, 0)
        slot_out[pl.ds(pl.multiple_of(s * 8, 8), 8), :] = jnp.where(half, to_right, to_left)

    even = (khi_even, klo_even, thi_even, tlo_even)
    odd = (khi_odd, klo_odd, thi_odd, tlo_odd)

    def evaluate_and_multiply(t, carry):
        before = jnp.maximum(t - 1, 0)
        product(2 * before, even, before)
        evaluate(2 * t, even, stage_even, t)
        product(2 * before + 1, odd, before)
        evaluate(jnp.minimum(2 * t + 1, SLOTS - 1), odd, stage_odd, t)
        return carry

    def products(g, carry):
        for u in range(GROUP):
            at = g * GROUP + u
            product(2 * at, even, at)
            product(2 * at + 1, odd, at)
        return carry

    for it in range(ITERS):
        if it == 0:
            lax.fori_loop(0, SLOTS // 2 + 1, evaluate_and_multiply, 0)
        else:
            lax.fori_loop(0, SLOTS // 2 // GROUP, products, 0)
        product(SLOTS - 1, even, SLOTS // 2)
        high, low = split(slot_out[...])
        table = onehot[...]
        added = dot_bf16(table, high, False) + dot_bf16(table, low, False)
        for d in range(9):
            part[it, d] = added[d * ROWS : (d + 1) * ROWS]
        arrive = exchange(
            lambda d: part.at[it, d],
            lambda d, at: got.at[it, at],
            fold_send.at[it],
            fold_recv.at[it],
        )
        image = part[it, 4]
        for at in range(8):
            arrive(at)
            image = image + got[it, at]
        for h in range(2):
            basis[it + 1, h] = image[:, 128 * h : 128 * h + 128]
        if it + 1 < ITERS:
            nearq[it, 4] = image
            arrive = exchange(
                lambda d: nearq.at[it, 4],
                lambda d, at: nearq.at[it, d],
                q_send.at[it],
                q_recv.at[it],
            )

            def refresh(d):
                for k in range(0, BLOCKS, 2):
                    value = nearq[it, d, 4 * k : 4 * k + 8, :]
                    put_pieces(d * BLOCKS + k, 0, value)
                    if k + 1 < BLOCKS:
                        put_pieces(d * BLOCKS + k + 1, 4, value)

            def refresh_next(at, carry):
                arrive(at)
                refresh(at + at // 4)
                return carry

            refresh(4)
            lax.fori_loop(0, 8, refresh_next, 0)

    lane = lax.broadcasted_iota(jnp.int32, (8, 128), 1)
    forward = lax.broadcasted_iota(jnp.int32, (8, 128), 0) % 4 < 2

    def swapped(value):
        return jnp.where(forward, pltpu.roll(value, 6, 0), pltpu.roll(value, 2, 0))

    tiles = [
        [basis[i, h, g : g + 8, :] for h in range(2) for g in range(0, ROWS, 8)]
        for i in range(ITERS + 1)
    ]
    crossed = [[swapped(tile) for tile in row] for row in tiles]
    places = {}
    gram = jnp.zeros((8, 128), F32)
    for i in range(ITERS + 1):
        for j in range(i, ITERS + 1):
            for kind, other in (("same", tiles), ("cross", crossed)):
                total = None
                for mine, theirs in zip(tiles[i], other[j]):
                    term = mine * theirs
                    total = term if total is None else total + term
                column = jnp.sum(total, axis=1, keepdims=True)
                places[kind, i, j] = len(places)
                gram = jnp.where(lane == places[kind, i, j], column, gram)

    for stage, group_peers in enumerate(peers):
        sums[stage] = gram
        copies = []
        for at, device in enumerate(group_peers):
            copy = pltpu.make_async_remote_copy(
                src_ref=sums.at[stage],
                dst_ref=sum_in.at[stage, at],
                send_sem=sum_send.at[stage, at],
                recv_sem=sum_recv.at[stage, at],
                device_id=device,
                device_id_type=MESH,
            )
            copy.start()
            copies.append(copy)
        pending.extend(copies)
        for at, copy in enumerate(copies):
            copy.wait_recv()
            gram = gram + sum_in[stage, at]
    gram = gram + pltpu.roll(gram, 4, 0)

    def entry(kind, i, j, second):
        value = jnp.broadcast_to(gram[:, places[kind, i, j] : places[kind, i, j] + 1], (8, 128))
        return pltpu.roll(value, 6, 0) if second else value

    chain = ITERS + 1
    inner = {}
    for i in range(chain):
        for j in range(chain):
            inner[i, j] = entry("same", min(i, j), max(i, j), False)
            if i < ITERS and j < ITERS:
                inner[chain + i, chain + j] = entry("same", min(i, j), max(i, j), True)
            if j < ITERS:
                cross = entry("cross", min(i, j), max(i, j), i > j)
                inner[i, chain + j] = cross
                inner[chain + j, i] = cross

    def bilinear(first, second):
        total = None
        for i, a in first.items():
            inside = None
            for j, b in second.items():
                term = b * inner[i, j]
                inside = term if inside is None else inside + term
            inside = a * inside
            total = inside if total is None else total + inside
        return total

    def combine(base, scale, other):
        result = dict(base)
        for i, value in other.items():
            result[i] = result[i] + scale * value if i in result else scale * value
        return result

    one = jnp.ones((8, 128), F32)
    in_x, in_r, in_p = {}, {chain: one}, {0: one}
    norm_now = inner[chain, chain]
    for it in range(ITERS):
        image = {i + 1: value for i, value in in_p.items()}
        step = norm_now / bilinear(in_p, image)
        in_x = combine(in_x, step, in_p)
        in_r = combine(in_r, -step, image)
        norm_next = bilinear(in_r, in_r)
        in_p = combine(in_r, norm_next / norm_now, in_p)
        norm_now = norm_next

    for f, h in ((0, 0), (0, 1), (1, 0), (1, 1)):
        lanes = slice(128 * h, 128 * h + 128)
        vectors = {}
        for i in range(chain):
            vectors[i] = basis[i, h, pl.ds(f, BLOCKS, stride=4), :]
            if i < ITERS:
                vectors[chain + i] = basis[i, h, pl.ds(2 + f, BLOCKS, stride=4), :]

        def mixed(total, coefficients):
            for i, value in coefficients.items():
                term = value[f : f + 1, :] * vectors[i]
                total = term if total is None else total + term
            return total

        results = (mixed(None, in_x), mixed(None, in_r), mixed(None, in_p))
        for k in range(BLOCKS):
            at = f * BLOCKS + k
            new_sol_ref[at, :, lanes] = sol_rows[at, :, lanes] + results[0][k : k + 1, :]
            new_res_ref[at, :, lanes] = results[1][k : k + 1, :]
            new_dir_ref[at, :, lanes] = results[2][k : k + 1, :]

    for copy in pending:
        copy.wait_send()


INNER = 29
OUTER = 32
INNER_FOURS = INNER // 4
OUTER_FOURS = OUTER // 4
INNER_WIDTH = 512
FAST_WIDTH = INNER_WIDTH + 8 * OUTER
FAST_TABLE = 64
P_ROWS = 24


def fast_body(
    sizes,
    stages,
    coord_ref,
    sol_ref,
    res_ref,
    dir_ref,
    pairs_hbm_ref,
    count_ref,
    new_sol_ref,
    new_res_ref,
    new_dir_ref,
    flag_ref,
    pairs_out_ref,
    own0,
    near0,
    nearq,
    nearp,
    khi_0,
    khi_1,
    khi_2,
    khi_3,
    klo_0,
    klo_1,
    klo_2,
    klo_3,
    own_pieces,
    pieces,
    slot_out,
    onehot,
    basis,
    sums,
    sum_in,
    raw,
    sol_rows,
    pairs_vec_ref,
    own_columns,
    lists,
    inner_rows,
    outer_rows,
    inner_entries,
    outer_entries,
    load_sems,
    entry_sems,
    list_send,
    list_recv,
    near_send,
    near_recv,
    q_send,
    q_recv,
    sum_send,
    sum_recv,
):
    wide_size, narrow_size = sizes
    wide = lax.axis_index("wide")
    narrow = lax.axis_index("narrow")
    neighbours = []
    for d in range(9):
        if d != 4:
            to_wide = (wide + (d // 3 - 1) + wide_size) % wide_size
            to_narrow = (narrow + (d % 3 - 1) + narrow_size) % narrow_size
            neighbours.append((d, (to_wide, to_narrow)))
    peers = stage_peers(wide, narrow, stages)

    loads = [
        pltpu.make_async_copy(source, landing, load_sems.at[at])
        for at, (source, landing) in enumerate(
            (
                (pairs_hbm_ref, pairs_vec_ref),
                (dir_ref, raw.at[pl.ds(0, 2 * BLOCKS)]),
                (res_ref, raw.at[pl.ds(2 * BLOCKS, 2 * BLOCKS)]),
                (coord_ref, raw.at[pl.ds(4 * BLOCKS, 3 * BLOCKS)]),
                (sol_ref, sol_rows),
            )
        )
    ]
    for load in loads:
        load.start()

    barrier = pltpu.get_barrier_semaphore()
    targets = [device for _, device in neighbours] + [device for group in peers for device in group]
    for device in targets:
        pl.semaphore_signal(barrier, inc=1, device_id=device, device_id_type=MESH)

    for load in loads:
        load.wait()
    pairs_out_ref[...] = pairs_vec_ref[...]
    live = lax.broadcasted_iota(jnp.int32, (2, SLOTS), 1) < count_ref[0:1, 0:1]
    own_list = jnp.where(live, pairs_vec_ref[...], 255).astype(F32)
    own_list = jnp.concatenate([own_list, jnp.full((2, 128 - SLOTS), 255.0, F32)], axis=1)
    lists[4] = jnp.concatenate([own_list, jnp.full((6, 128), 255.0, F32)], axis=0)
    for k in range(BLOCKS):
        for c in range(7):
            own0[k, c : c + 1, :] = raw[c * BLOCKS + k]
        own0[k, 7:8, :] = jnp.zeros((1, NODES), F32)

    pl.semaphore_wait(barrier, len(targets))

    pending = []

    def exchange(source, landing, send_sem, recv_sem):
        for at, (d, device) in enumerate(neighbours):
            copy = pltpu.make_async_remote_copy(
                src_ref=source,
                dst_ref=landing(8 - d),
                send_sem=send_sem.at[at],
                recv_sem=recv_sem.at[7 - at],
                device_id=device,
                device_id_type=MESH,
            )
            copy.start()
            pending.append(copy)

        def wait(at):
            pltpu.make_async_remote_copy(
                src_ref=source,
                dst_ref=landing(at + at // 4),
                send_sem=send_sem.at[at],
                recv_sem=recv_sem.at[at],
                device_id=neighbours[0][1],
                device_id_type=MESH,
            ).wait_recv()

        return wait

    list_arrive = exchange(lists.at[4], lambda d: lists.at[d], list_send, list_recv)
    near_arrive = exchange(
        own0,
        lambda d: near0.at[pl.ds(d * BLOCKS, BLOCKS)],
        near_send,
        near_recv,
    )

    half = lax.broadcasted_iota(jnp.int32, (8, NODES), 0) < 4

    def put_pieces(to, j, rows_at, value):
        high = value.astype(BF16).astype(F32)
        low = value - high
        if rows_at == 0:
            rows = jnp.where(half, high, pltpu.roll(low, 4, 0))
        else:
            rows = jnp.where(half, pltpu.roll(high, 4, 0), low)
        to[j] = jnp.concatenate([rows, rows], axis=0).astype(BF16)

    for h in range(2):
        for k in range(BLOCKS):
            basis[0, h, 4 * k : 4 * k + 4, :] = own0[k, 0:4, 128 * h : 128 * h + 128]
        basis[0, h, 4 * BLOCKS : ROWS, :] = jnp.zeros((ROWS - 4 * BLOCKS, 128), F32)


    before_lane = lax.broadcasted_iota(jnp.int32, (128, 128), 0) < lax.broadcasted_iota(
        jnp.int32, (128, 128), 1
    )
    before_lane = jnp.where(before_lane, 1.0, 0.0).astype(BF16)
    entry_of = lax.broadcasted_iota(jnp.int32, (128, 128), 0).astype(F32)
    row_of = lax.broadcasted_iota(jnp.int32, (8, 128), 0)

    def compact(wanted_rows, codes, rows, most_entries):
        count = wanted_rows.shape[0]
        before_row = lax.broadcasted_iota(jnp.int32, (count, count), 0) > lax.broadcasted_iota(
            jnp.int32, (count, count), 1
        )
        in_row = dot_bf16(wanted_rows.astype(BF16), before_lane, False)
        row_total = jnp.broadcast_to(jnp.sum(wanted_rows, axis=1, keepdims=True), (count, 128))
        rank = in_row + dot_bf16(
            jnp.where(before_row, 1.0, 0.0).astype(BF16), row_total.astype(BF16), False
        )
        everything = jnp.sum(row_total, axis=0, keepdims=True)
        rank = jnp.where(wanted_rows > 0.5, rank, -1.0)
        gathered = jnp.zeros((128, 128), F32)
        for row in rows:
            gathered = gathered + jnp.where(
                entry_of == rank[row : row + 1, :], codes[row : row + 1, :], 0.0
            )
        gathered = jnp.broadcast_to(jnp.sum(gathered, axis=1, keepdims=True), (128, 128))
        code = jnp.transpose(gathered)[0:8, :].astype(jnp.int32)
        return code, jnp.where(everything > most_entries + 0.5, 1.0, 0.0)

    def fill_onehot(start, wanted):
        width = wanted.shape[1]
        for first in range(0, FAST_TABLE, CHUNK):
            row = lax.broadcasted_iota(jnp.int32, (CHUNK, width), 0) + first
            lane = lax.broadcasted_iota(jnp.int32, (CHUNK, width), 1)
            second = row - ROWS
            block = jnp.where(row < ROWS, row >> 2, second >> 1)
            vector = jnp.where(row < ROWS, row & 3, second & 1)
            match = (block == wanted) & (vector == (lane & 3))
            onehot[first : first + CHUNK, start : start + width] = jnp.where(
                match, 1.0, 0.0
            ).astype(BF16)

    def spread_over(targets_rows, width, shift):
        entry_row = lax.broadcasted_iota(jnp.int32, (128, width), 0)
        entry_lane = lax.broadcasted_iota(jnp.int32, (128, width), 1) >> shift
        spread = jnp.where(entry_row == entry_lane, 1.0, 0.0).astype(BF16)
        return dot_bf16(targets_rows.astype(F32).astype(BF16), spread, False).astype(jnp.int32)

    own_ids = lists[4]
    own_left = jnp.broadcast_to(own_ids[0:1, :], (8, 128)) - 4.0 * BLOCKS
    own_right = jnp.broadcast_to(own_ids[1:2, :], (8, 128)) - 4.0 * BLOCKS
    inside = (own_left > -0.5) & (own_left < BLOCKS - 0.5) & (own_right > -0.5) & (own_right < BLOCKS - 0.5)
    code, overflow = compact(
        jnp.where(inside & (row_of == 0), 1.0, 0.0), own_left * 128.0 + own_right + 1.0, (0,), INNER
    )
    filled = code > 0
    code = jnp.maximum(code - 1, 0)
    inner_left, inner_right = code >> 7, code & 127
    inner_rows[...] = jnp.where(row_of == 0, inner_left, inner_right)
    inner_load = pltpu.make_async_copy(inner_rows, inner_entries, entry_sems.at[0])
    inner_load.start()

    def own_block(k, carry):
        value = own0[k]
        put_pieces(own_pieces, k, 0, value)
        turned = jnp.transpose(value)
        for axis in range(3):
            own_columns[k, axis] = jnp.broadcast_to(turned[:, 4 + axis : 5 + axis], (NODES, 128))
        return carry

    lax.fori_loop(0, BLOCKS, own_block, 0)

    ends = jnp.where(row_of == 0, inner_left, inner_right)
    ends = jnp.where(filled & ((row_of == 0) | (inner_left != inner_right)), ends, 200)
    wanted = spread_over(ends, INNER_WIDTH, 4)
    lane = lax.broadcasted_iota(jnp.int32, (1, INNER_WIDTH), 1)
    fill_onehot(0, jnp.where((lane & 8) == 0, wanted[0:1, :], wanted[1:2, :]))
    inner_load.wait()

    def evaluate(block, other, refs, at):
        high_ref, low_ref = refs
        block = jnp.clip(block, 0, BLOCKS - 1)
        for h in range(2):
            lanes = slice(128 * h, 128 * h + 128)
            others = [
                jnp.broadcast_to(other[4 + axis : 5 + axis, lanes], (CHUNK, 128)) for axis in range(3)
            ]
            for first in range(0, NODES, CHUNK):
                squared = None
                for axis in range(3):
                    offset = own_columns[block, axis, first : first + CHUNK, :] - others[axis]
                    squared = offset * offset if squared is None else squared + offset * offset
                squared = jnp.minimum(squared, RADIUS * RADIUS)
                distance = squared * lax.rsqrt(jnp.maximum(squared, 1e-36))
                rest = RADIUS - distance
                rest = rest * rest
                rest = rest * rest
                high, low = split(rest * (PHI_SLOPE * distance + PHI_CONST))
                high_ref[at, first : first + CHUNK, lanes] = high
                low_ref[at, first : first + CHUNK, lanes] = low

    def evaluate_inner(e, refs, at):
        other = own0[jnp.clip(inner_entries[1, e], 0, BLOCKS - 1)]
        evaluate(inner_entries[0, e], other, refs, at)

    def evaluate_outer(e, refs, at):
        other = near0[jnp.clip(outer_entries[1, e], 0, 9 * BLOCKS - 1)]
        evaluate(outer_entries[0, e], other, refs, at)

    def product_inner(e, refs, at):
        high, low = refs[0][at], refs[1][at]
        left = own_pieces[jnp.clip(inner_entries[0, e], 0, BLOCKS - 1)]
        right = own_pieces[jnp.clip(inner_entries[1, e], 0, BLOCKS - 1)]
        to_left = dot_bf16(right, high, True) + dot_bf16(right, low, True)
        to_right = dot_bf16(left, high, False) + dot_bf16(left, low, False)
        start = pl.multiple_of(e * 16, 16)
        slot_out[pl.ds(start, 8), :] = to_left[0:8]
        slot_out[pl.ds(start + 8, 8), :] = to_right[0:8]

    def product_outer(e, refs, at):
        other = pieces[jnp.clip(outer_entries[1, e], 0, 9 * BLOCKS - 1)]
        result = dot_bf16(other, refs[0][at], True) + dot_bf16(other, refs[1][at], True)
        slot_out[pl.ds(pl.multiple_of(INNER_WIDTH + e * 8, 8), 8), :] = result[0:8]

    tiles_of = ((khi_0, klo_0), (khi_1, klo_1), (khi_2, klo_2), (khi_3, klo_3))

    def evaluate_and_multiply(evaluate_one, product_one, start, fours):
        def step(t, carry):
            before = jnp.maximum(t - 1, 0)
            for u, refs in enumerate(tiles_of):
                product_one(4 * before + u, refs, start + before)
                evaluate_one(4 * t + u, refs, start + t)
            return carry

        lax.fori_loop(0, fours, step, 0)

    def last_four(product_one, start, fours):
        for u, refs in enumerate(tiles_of):
            product_one(4 * (fours - 1) + u, refs, start + fours - 1)

    def multiply(product_one, start, fours, group):
        def step(g, carry):
            for at in range(group):
                for u, refs in enumerate(tiles_of):
                    product_one(4 * (g * group + at) + u, refs, start + g * group + at)
            return carry

        lax.fori_loop(0, fours // group, step, 0)

    slot_out[16 * INNER : INNER_WIDTH, :] = jnp.zeros((INNER_WIDTH - 16 * INNER, NODES), F32)
    evaluate_and_multiply(evaluate_inner, product_inner, 0, INNER_FOURS)
    for at in range(8):
        list_arrive(at)
    evaluate_inner(INNER - 1, tiles_of[0], INNER_FOURS)
    last_four(product_inner, 0, INNER_FOURS)

    dead_rows = jnp.full((7, 128), 255.0, F32)
    device_row = lax.broadcasted_iota(jnp.int32, (16, 128), 0)
    add_wide = (device_row * 11 >> 5) - 1
    add_narrow = device_row - (add_wide + 1) * 3 - 1

    def here(row):
        ids = jnp.concatenate([lists[d, row : row + 1, :] for d in range(9)] + [dead_rows], axis=0)
        ids = ids.astype(jnp.int32)
        is_live = ids < 200
        ids = jnp.where(is_live, ids, 0)
        device = ids * 7282 >> 16
        within = ids - device * 9
        at_wide = device * 11 >> 5
        at_narrow = device - at_wide * 3 + add_narrow
        at_wide = at_wide + add_wide
        mine = is_live & (at_wide == 1) & (at_narrow == 1)
        return mine, within, at_wide * 27 + at_narrow * 9 + within

    left_mine, left_within, left_here = here(0)
    right_mine, right_within, right_here = here(1)
    wanted_rows = jnp.concatenate(
        [
            jnp.where(left_mine & jnp.logical_not(right_mine), 1.0, 0.0),
            jnp.where(right_mine & jnp.logical_not(left_mine), 1.0, 0.0),
        ],
        axis=0,
    )
    codes = jnp.concatenate(
        [left_within * 128 + right_here + 1, right_within * 128 + left_here + 1], axis=0
    ).astype(F32)
    code, too_many = compact(wanted_rows, codes, (*range(9), *range(16, 25)), OUTER)
    overflow = overflow + too_many
    filled = code > 0
    code = jnp.maximum(code - 1, 0)
    outer_rows[...] = jnp.where(row_of == 0, code >> 7, code & 127)
    outer_load = pltpu.make_async_copy(outer_rows, outer_entries, entry_sems.at[1])
    outer_load.start()
    fill_onehot(INNER_WIDTH, spread_over(jnp.where(filled, code >> 7, 200), 8 * OUTER, 3)[0:1, :])

    product_inner(INNER - 1, tiles_of[0], INNER_FOURS)

    def prepare_next(at, carry):
        near_arrive(at)
        for k in range(BLOCKS):
            j = (at + at // 4) * BLOCKS + k
            put_pieces(pieces, j, 0, near0[j])
        return carry

    lax.fori_loop(0, 8, prepare_next, 0)
    outer_load.wait()
    evaluate_and_multiply(evaluate_outer, product_outer, INNER_FOURS + 1, OUTER_FOURS)
    last_four(product_outer, INNER_FOURS + 1, OUTER_FOURS)

    lane = lax.broadcasted_iota(jnp.int32, (8, 128), 1)
    forward = row_of % 4 < 2
    places = {}

    def swapped(value):
        return jnp.where(forward, pltpu.roll(value, 6, 0), pltpu.roll(value, 2, 0))

    def add_products(gram, j):
        tiles = [
            [basis[i, h, g : g + 8, :] for h in range(2) for g in range(0, ROWS, 8)] for i in range(j + 1)
        ]
        crossed = [swapped(tile) for tile in tiles[j]]
        for i in range(j + 1):
            for kind, others in (("same", tiles[j]), ("cross", crossed)):
                total = None
                for mine, theirs in zip(tiles[i], others):
                    term = mine * theirs
                    total = term if total is None else total + term
                column = jnp.sum(total, axis=1, keepdims=True)
                places[kind, i, j] = len(places)
                gram = jnp.where(lane == places[kind, i, j], column, gram)
        return gram

    gram = jnp.zeros((8, 128), F32)
    for it in range(ITERS):
        if it > 0:
            gram = add_products(gram, it - 1)
            if it + 1 == ITERS:
                gram = add_products(gram, it)
            multiply(product_inner, 0, INNER_FOURS, 1)
            product_inner(INNER - 1, tiles_of[0], INNER_FOURS)
            refresh_others()
            multiply(product_outer, INNER_FOURS + 1, OUTER_FOURS, 2)
        high, low = split(slot_out[...])
        table = onehot[...]
        image = dot_bf16(table, high, False) + dot_bf16(table, low, False)
        for h in range(2):
            basis[it + 1, h] = image[0:ROWS, 128 * h : 128 * h + 128]
        if it == 0:
            nearq[4] = image[0:ROWS]
            arrive = exchange(nearq.at[4], lambda d: nearq.at[d], q_send.at[it], q_recv.at[it])

            def refresh(d, to, first_block):
                for k in range(0, BLOCKS, 2):
                    value = nearq[d, 4 * k : 4 * k + 8, :]
                    put_pieces(to, first_block + k, 0, value)
                    if k + 1 < BLOCKS:
                        put_pieces(to, first_block + k + 1, 4, value)

            refresh(4, own_pieces, 0)

            def refresh_others(arrive=arrive, refresh=refresh):
                def refresh_next(at, carry):
                    arrive(at)
                    d = at + at // 4
                    refresh(d, pieces, d * BLOCKS)
                    return carry

                lax.fori_loop(0, 8, refresh_next, 0)

        elif it + 1 < ITERS:
            nearp[4] = image[ROWS : ROWS + P_ROWS]
            arrive_p = exchange(nearp.at[4], lambda d: nearp.at[d], q_send.at[it], q_recv.at[it])

            def refresh_p(d, to, first_block):
                for k in range(BLOCKS):
                    value = nearp[d, k // 4 * 8 : k // 4 * 8 + 8, :]
                    if k % 4:
                        value = pltpu.roll(value, 8 - k % 4 * 2, 0)
                    put_pieces(to, first_block + k, 0, value)

            refresh_p(4, own_pieces, 0)

            def refresh_others(arrive=arrive_p, refresh=refresh_p):
                def refresh_next(at, carry):
                    arrive(at)
                    d = at + at // 4
                    refresh(d, pieces, d * BLOCKS)
                    return carry

                lax.fori_loop(0, 8, refresh_next, 0)

    gram = add_products(gram, ITERS)
    gram = jnp.where(lane == 127, overflow, gram)

    for stage, group_peers in enumerate(peers):
        sums[stage] = gram
        copies = []
        for at, device in enumerate(group_peers):
            copy = pltpu.make_async_remote_copy(
                src_ref=sums.at[stage],
                dst_ref=sum_in.at[stage, at],
                send_sem=sum_send.at[stage, at],
                recv_sem=sum_recv.at[stage, at],
                device_id=device,
                device_id_type=MESH,
            )
            copy.start()
            copies.append(copy)
        pending.extend(copies)
        for at, copy in enumerate(copies):
            copy.wait_recv()
            gram = gram + sum_in[stage, at]
    flag_ref[0, 0] = jnp.sum(jnp.where((lane == 127) & (half[:, 0:128]), gram, 0.0))
    gram = gram + pltpu.roll(gram, 4, 0)

    def entry(kind, i, j, second):
        value = jnp.broadcast_to(gram[:, places[kind, i, j] : places[kind, i, j] + 1], (8, 128))
        return pltpu.roll(value, 6, 0) if second else value

    chain = ITERS + 1
    inner = {}
    for i in range(chain):
        for j in range(chain):
            inner[i, j] = entry("same", min(i, j), max(i, j), False)
            if i < ITERS and j < ITERS:
                inner[chain + i, chain + j] = entry("same", min(i, j), max(i, j), True)
            if j < ITERS:
                cross = entry("cross", min(i, j), max(i, j), i > j)
                inner[i, chain + j] = cross
                inner[chain + j, i] = cross

    def bilinear(first, second):
        total = None
        for i, a in first.items():
            inside = None
            for j, b in second.items():
                term = b * inner[i, j]
                inside = term if inside is None else inside + term
            inside = a * inside
            total = inside if total is None else total + inside
        return total

    def combine(base, scale, other):
        result = dict(base)
        for i, value in other.items():
            result[i] = result[i] + scale * value if i in result else scale * value
        return result

    one = jnp.ones((8, 128), F32)
    in_x, in_r, in_p = {}, {chain: one}, {0: one}
    norm_now = inner[chain, chain]
    for it in range(ITERS):
        image = {i + 1: value for i, value in in_p.items()}
        step = norm_now / bilinear(in_p, image)
        in_x = combine(in_x, step, in_p)
        in_r = combine(in_r, -step, image)
        norm_next = bilinear(in_r, in_r)
        in_p = combine(in_r, norm_next / norm_now, in_p)
        norm_now = norm_next

    for f, h in ((0, 0), (0, 1), (1, 0), (1, 1)):
        lanes = slice(128 * h, 128 * h + 128)
        vectors = {}
        for i in range(chain):
            vectors[i] = basis[i, h, pl.ds(f, BLOCKS, stride=4), :]
            if i < ITERS:
                vectors[chain + i] = basis[i, h, pl.ds(2 + f, BLOCKS, stride=4), :]

        def mixed(total, coefficients):
            for i, value in coefficients.items():
                term = value[f : f + 1, :] * vectors[i]
                total = term if total is None else total + term
            return total

        results = (mixed(None, in_x), mixed(None, in_r), mixed(None, in_p))
        for k in range(BLOCKS):
            at = f * BLOCKS + k
            new_sol_ref[at, :, lanes] = sol_rows[at, :, lanes] + results[0][k : k + 1, :]
            new_res_ref[at, :, lanes] = results[1][k : k + 1, :]
            new_dir_ref[at, :, lanes] = results[2][k : k + 1, :]

    for copy in pending:
        copy.wait_send()


def hand_out(*refs):
    sems = refs[6]
    copies = [pltpu.make_async_copy(refs[i], refs[3 + i], sems.at[i]) for i in range(3)]
    for copy in copies:
        copy.start()
    for copy in copies:
        copy.wait()


def solution(mesh):
    sizes = (mesh.shape["wide"], mesh.shape["narrow"])
    if sizes[0] == 64:
        stages = (
            ("narrow", ((1, sizes[1]),)),
            ("wide", ((2, 8),)),
            ("wide", ((16, 4), (1, 2))),
        )
    else:
        stages = (("narrow", ((1, sizes[1]),)), ("wide", ((1, sizes[0]),)))
    most = 0
    for _, places in stages:
        size = 1
        for _, count in places:
            size *= count
        most = max(most, size - 1)

    def on_device(node_coords, solution, residual, direction, tile_pairs, tile_counts):
        full_shape = direction.shape
        fields = jax.ShapeDtypeStruct((2 * BLOCKS, 1, NODES), F32)
        vmem = pl.BlockSpec(memory_space=pltpu.VMEM)
        anywhere = pl.BlockSpec(memory_space=pl.ANY)
        dma = pltpu.SemaphoreType.DMA
        fast = pl.pallas_call(
            functools.partial(fast_body, sizes, stages),
            out_shape=(fields, fields, fields, jax.ShapeDtypeStruct((1, 1), F32), jax.ShapeDtypeStruct((2, SLOTS), jnp.int32)),
            in_specs=[anywhere] * 5 + [vmem],
            out_specs=(vmem, vmem, vmem, pl.BlockSpec(memory_space=pltpu.SMEM), vmem),
            scratch_shapes=[
                pltpu.VMEM((BLOCKS, 8, NODES), F32),
                pltpu.VMEM((9 * BLOCKS, 8, NODES), F32),
                pltpu.VMEM((9, ROWS, NODES), F32),
                pltpu.VMEM((9, P_ROWS, NODES), F32),
                *[pltpu.VMEM((INNER_FOURS + 1 + OUTER_FOURS, NODES, NODES), BF16)] * 8,
                pltpu.VMEM((BLOCKS, 16, NODES), BF16),
                pltpu.VMEM((9 * BLOCKS, 16, NODES), BF16),
                pltpu.VMEM((FAST_WIDTH, NODES), F32),
                pltpu.VMEM((FAST_TABLE, FAST_WIDTH), BF16),
                pltpu.VMEM((ITERS + 1, 2, ROWS, 128), F32),
                pltpu.VMEM((len(stages), 8, 128), F32),
                pltpu.VMEM((len(stages), most, 8, 128), F32),
                pltpu.VMEM((7 * BLOCKS, 1, NODES), F32),
                pltpu.VMEM((2 * BLOCKS, 1, NODES), F32),
                pltpu.VMEM((2, SLOTS), jnp.int32),
                pltpu.VMEM((BLOCKS, 3, NODES, 128), F32),
                pltpu.VMEM((9, 8, 128), F32),
                pltpu.VMEM((8, 128), jnp.int32),
                pltpu.VMEM((8, 128), jnp.int32),
                pltpu.SMEM((8, 128), jnp.int32),
                pltpu.SMEM((8, 128), jnp.int32),
                dma((5,)),
                dma((2,)),
                dma((8,)),
                dma((8,)),
                dma((8,)),
                dma((8,)),
                dma((ITERS - 1, 8)),
                dma((ITERS - 1, 8)),
                dma((len(stages), most)),
                dma((len(stages), most)),
            ],
            compiler_params=pltpu.CompilerParams(
                collective_id=0, has_side_effects=True, vmem_limit_bytes=60 * 1024 * 1024
            ),
            cost_estimate=pl.CostEstimate(
                flops=81 * 65536 * 40, bytes_accessed=200000, transcendentals=81 * 65536
            ),
        )
        general = pl.pallas_call(
            functools.partial(general_body, sizes, stages),
            out_shape=(fields, fields, fields),
            in_specs=[anywhere] * 5 + [vmem],
            out_specs=(vmem, vmem, vmem),
            scratch_shapes=[
                pltpu.VMEM((9 * BLOCKS, 8, NODES), F32),
                pltpu.VMEM((ITERS - 1, 9, ROWS, NODES), F32),
                pltpu.VMEM((ITERS, 9, ROWS, NODES), F32),
                pltpu.VMEM((ITERS, 8, ROWS, NODES), F32),
                pltpu.VMEM((SLOTS // 2 + 1, NODES, NODES), BF16),
                pltpu.VMEM((SLOTS // 2 + 1, NODES, NODES), BF16),
                pltpu.VMEM((SLOTS // 2 + 1, NODES, NODES), BF16),
                pltpu.VMEM((SLOTS // 2 + 1, NODES, NODES), BF16),
                pltpu.VMEM((SLOTS // 2 + 1, NODES, NODES), BF16),
                pltpu.VMEM((SLOTS // 2 + 1, NODES, NODES), BF16),
                pltpu.VMEM((SLOTS // 2 + 1, NODES, NODES), BF16),
                pltpu.VMEM((SLOTS // 2 + 1, NODES, NODES), BF16),
                pltpu.VMEM((NODES, NODES), F32),
                pltpu.VMEM((NODES, NODES), F32),
                pltpu.VMEM((9 * BLOCKS, 16, NODES), BF16),
                pltpu.VMEM((512, NODES), F32),
                pltpu.VMEM((TABLE, 512), BF16),
                pltpu.VMEM((ITERS + 1, 2, ROWS, 128), F32),
                pltpu.VMEM((len(stages), 8, 128), F32),
                pltpu.VMEM((len(stages), most, 8, 128), F32),
                pltpu.VMEM((7 * BLOCKS, 1, NODES), F32),
                pltpu.VMEM((2 * BLOCKS, 1, NODES), F32),
                pltpu.SMEM((2, SLOTS), jnp.int32),
                pltpu.VMEM((2, SLOTS), jnp.int32),
                pltpu.VMEM((9 * BLOCKS, NODES, 8), F32),
                dma((6,)),
                dma((8,)),
                dma((8,)),
                dma((ITERS - 1, 8)),
                dma((ITERS - 1, 8)),
                dma((ITERS, 8)),
                dma((ITERS, 8)),
                dma((len(stages), most)),
                dma((len(stages), most)),
            ],
            compiler_params=pltpu.CompilerParams(
                collective_id=1, has_side_effects=True, vmem_limit_bytes=60 * 1024 * 1024
            ),
            cost_estimate=pl.CostEstimate(
                flops=61 * 65536 * 40, bytes_accessed=200000, transcendentals=61 * 65536
            ),
        )
        arguments = (
            node_coords.reshape(3 * BLOCKS, 1, NODES),
            solution.reshape(2 * BLOCKS, 1, NODES),
            residual.reshape(2 * BLOCKS, 1, NODES),
            direction.reshape(2 * BLOCKS, 1, NODES),
            tile_pairs.reshape(2, SLOTS),
            tile_counts,
        )
        *outs, flags, pairs = fast(*arguments)
        outs = lax.cond(
            flags[0, 0] > 0.5,
            lambda *a: tuple(general(*a[3:])),
            lambda *a: a[:3],
            *outs,
            *arguments[:4],
            pairs,
            arguments[5],
        )
        outs = pl.pallas_call(
            hand_out,
            out_shape=(fields, fields, fields),
            in_specs=[anywhere] * 3,
            out_specs=(anywhere,) * 3,
            scratch_shapes=[dma((3,))],
        )(*outs)
        return tuple(out.reshape(full_shape) for out in outs)

    fields_spec = P(None, "wide", "narrow", None, None)
    return jax.shard_map(
        on_device,
        mesh=mesh,
        in_specs=(
            fields_spec,
            fields_spec,
            fields_spec,
            fields_spec,
            P("wide", "narrow", None, None),
            P("wide", "narrow"),
        ),
        out_specs=(fields_spec, fields_spec, fields_spec),
        check_vma=False,
    )
```

profile of v0, /device:TPU:1, one launch (start us, length us, event | category | flops | bytes accessed | tf_op | source)
XLA Modules:
  0.0 67.7 jit_solution(15349978319643654271)
XLA Ops:
  1.3 0.0 copy-start
  1.3 0.0 copy-start.1
  1.3 0.0 copy-start.2
  1.3 0.0 copy-start.3
  1.3 65.0 %shard_map.85 = (f32[18,1,256]{2,1,0:T(1,128)S(1)}, f32[18,1,256]{2,1,0:T(1,128)S(1)}, f32[18,1,256]{2,1,0:T(1,128)S(1)}, f32[1,1]{1,0:T(1,128)}, s32[2,61]{1,0:T(2,128)S(1)}) custom-call(f32[27,1,256]{2,1,0:T(1,128)} %bitcast.15, f32[18,1,256]{2,1,0:T(1,128)} %bitcast.17, f32[18,1,256]{2,1,0:T(1,128)} %bitcast.19, f32[18,1,256]{2,1,0:T(1,128)} %bitcast.21, ...), custom_call_target="tpu_custom_call" | custom-call | flops 212336640 | bytes 200000 | tf_op jit(solution)/shard_map/pallas_call | solution.py:1132
  67.0 0.0 copy-done
  67.1 0.0 copy-done.1
  67.1 0.0 copy-done.2
  67.1 0.0 copy-done.3
  67.1 0.6 shard_map.86
  (1 shorter events, 0.0 us)
Async XLA Ops:
  1.3 65.8 %copy-start = (f32[3,1,1,9,256]{4,2,3,1,0:T(1,128)S(1)}, f32[3,1,1,9,256]{4,2,3,1,0:T(1,128)}, u32[]{:S(2)}) copy-start(f32[3,1,1,9,256]{4,2,3,1,0:T(1,128)} %param.8) | copy-start | bytes 82948
  1.3 65.8 %copy-start.1 = (f32[2,1,1,9,256]{4,2,3,1,0:T(1,128)S(1)}, f32[2,1,1,9,256]{4,2,3,1,0:T(1,128)}, u32[]{:S(2)}) copy-start(f32[2,1,1,9,256]{4,2,3,1,0:T(1,128)} %param.9) | copy-start | bytes 55300
  1.3 65.8 %copy-start.2 = (f32[2,1,1,9,256]{4,2,3,1,0:T(1,128)S(1)}, f32[2,1,1,9,256]{4,2,3,1,0:T(1,128)}, u32[]{:S(2)}) copy-start(f32[2,1,1,9,256]{4,2,3,1,0:T(1,128)} %param.10) | copy-start | bytes 55300
  1.3 65.8 %copy-start.3 = (f32[2,1,1,9,256]{4,2,3,1,0:T(1,128)S(1)}, f32[2,1,1,9,256]{4,2,3,1,0:T(1,128)}, u32[]{:S(2)}) copy-start(f32[2,1,1,9,256]{4,2,3,1,0:T(1,128)} %param.11) | copy-start | bytes 55300
where the time goes:
time: 68 us; the launch traced here: 67.7 us
  Pallas kernels  65.7 us (97%)
  between operations  2.04 us (3%)
    pallas_call x1, Pallas kernels, on_device(): *outs, flags, pairs = fast(*arguments)  65 us

commit v1 on v0

--- a/solution.py
+++ b/solution.py
@@ -563,7 +563,8 @@
     pending = []
 
     def exchange(source, landing, send_sem, recv_sem):
-        for at, (d, device) in enumerate(neighbours):
+        for at in (0, 2, 5, 7, 3, 4, 1, 6):
+            d, device = neighbours[at]
             copy = pltpu.make_async_remote_copy(
                 src_ref=source,
                 dst_ref=landing(8 - d),
@@ -808,6 +809,13 @@
 
     product_inner(INNER - 1, tiles_of[0], INNER_FOURS)
 
+    def added(start, end):
+        high, low = split(slot_out[start:end, :])
+        table = onehot[:, start:end]
+        return dot_bf16(table, high, False) + dot_bf16(table, low, False)
+
+    inner_image = added(0, INNER_WIDTH)
+
     def prepare_next(at, carry):
         near_arrive(at)
         for k in range(BLOCKS):
@@ -851,11 +859,10 @@
                 gram = add_products(gram, it)
             multiply(product_inner, 0, INNER_FOURS, 1)
             product_inner(INNER - 1, tiles_of[0], INNER_FOURS)
+            inner_image = added(0, INNER_WIDTH)
             refresh_others()
             multiply(product_outer, INNER_FOURS + 1, OUTER_FOURS, 2)
-        high, low = split(slot_out[...])
-        table = onehot[...]
-        image = dot_bf16(table, high, False) + dot_bf16(table, low, False)
+        image = inner_image + added(INNER_WIDTH, FAST_WIDTH)
         for h in range(2):
             basis[it + 1, h] = image[0:ROWS, 128 * h : 128 * h + 128]
         if it == 0:
@@ -908,17 +915,19 @@
     for stage, group_peers in enumerate(peers):
         sums[stage] = gram
         copies = []
-        for at, device in enumerate(group_peers):
+        count = len(group_peers)
+        for at in sorted(range(count), key=lambda at: -min(at + 1, count - at)):
             copy = pltpu.make_async_remote_copy(
                 src_ref=sums.at[stage],
                 dst_ref=sum_in.at[stage, at],
                 send_sem=sum_send.at[stage, at],
                 recv_sem=sum_recv.at[stage, at],
-                device_id=device,
+                device_id=group_peers[at],
                 device_id_type=MESH,
             )
             copy.start()
-            copies.append(copy)
+            copies.append((at, copy))
+        copies = [copy for at, copy in sorted(copies, key=lambda pair: pair[0])]
         pending.extend(copies)
         for at, copy in enumerate(copies):
             copy.wait_recv()

time: 68 us -> 67.6 us (level)
  no operation moved by 1% of the time
where the time goes in v1:
time: 67.6 us; the launch traced here: 67.3 us
  Pallas kernels  65.3 us (97%)
  between operations  2.04 us (3%)
    pallas_call x1, Pallas kernels, on_device(): *outs, flags, pairs = fast(*arguments)  64.6 us

profile of v1, /device:TPU:1, one launch (start us, length us, event | category | flops | bytes accessed | tf_op | source)
XLA Modules:
  0.0 67.3 jit_solution(18019917804145453398)
XLA Ops:
  1.3 0.0 copy-start
  1.3 0.0 copy-start.1
  1.3 0.0 copy-start.2
  1.3 0.0 copy-start.3
  1.3 64.6 %shard_map.85 = (f32[18,1,256]{2,1,0:T(1,128)S(1)}, f32[18,1,256]{2,1,0:T(1,128)S(1)}, f32[18,1,256]{2,1,0:T(1,128)S(1)}, f32[1,1]{1,0:T(1,128)}, s32[2,61]{1,0:T(2,128)S(1)}) custom-call(f32[27,1,256]{2,1,0:T(1,128)} %bitcast.15, f32[18,1,256]{2,1,0:T(1,128)} %bitcast.17, f32[18,1,256]{2,1,0:T(1,128)} %bitcast.19, f32[18,1,256]{2,1,0:T(1,128)} %bitcast.21, ...), custom_call_target="tpu_custom_call" | custom-call | flops 212336640 | bytes 200000 | tf_op jit(solution)/shard_map/pallas_call | solution.py:1141
  66.6 0.0 copy-done
  66.6 0.0 copy-done.1
  66.6 0.0 copy-done.2
  66.7 0.0 copy-done.3
  66.7 0.6 shard_map.86
  (1 shorter events, 0.0 us)
Async XLA Ops:
  1.3 65.3 %copy-start = (f32[3,1,1,9,256]{4,2,3,1,0:T(1,128)S(1)}, f32[3,1,1,9,256]{4,2,3,1,0:T(1,128)}, u32[]{:S(2)}) copy-start(f32[3,1,1,9,256]{4,2,3,1,0:T(1,128)} %param.8) | copy-start | bytes 82948
  1.3 65.3 %copy-start.1 = (f32[2,1,1,9,256]{4,2,3,1,0:T(1,128)S(1)}, f32[2,1,1,9,256]{4,2,3,1,0:T(1,128)}, u32[]{:S(2)}) copy-start(f32[2,1,1,9,256]{4,2,3,1,0:T(1,128)} %param.9) | copy-start | bytes 55300
  1.3 65.3 %copy-start.2 = (f32[2,1,1,9,256]{4,2,3,1,0:T(1,128)S(1)}, f32[2,1,1,9,256]{4,2,3,1,0:T(1,128)}, u32[]{:S(2)}) copy-start(f32[2,1,1,9,256]{4,2,3,1,0:T(1,128)} %param.10) | copy-start | bytes 55300
  1.3 65.3 %copy-start.3 = (f32[2,1,1,9,256]{4,2,3,1,0:T(1,128)S(1)}, f32[2,1,1,9,256]{4,2,3,1,0:T(1,128)}, u32[]{:S(2)}) copy-start(f32[2,1,1,9,256]{4,2,3,1,0:T(1,128)} %param.11) | copy-start | bytes 55300

commit v2 on v1

--- a/solution.py
+++ b/solution.py
@@ -499,15 +499,12 @@
     sol_rows,
     pairs_vec_ref,
     own_columns,
-    lists,
     inner_rows,
     outer_rows,
     inner_entries,
     outer_entries,
     load_sems,
     entry_sems,
-    list_send,
-    list_recv,
     near_send,
     near_recv,
     q_send,
@@ -552,11 +549,12 @@
     live = lax.broadcasted_iota(jnp.int32, (2, SLOTS), 1) < count_ref[0:1, 0:1]
     own_list = jnp.where(live, pairs_vec_ref[...], 255).astype(F32)
     own_list = jnp.concatenate([own_list, jnp.full((2, 128 - SLOTS), 255.0, F32)], axis=1)
-    lists[4] = jnp.concatenate([own_list, jnp.full((6, 128), 255.0, F32)], axis=0)
     for k in range(BLOCKS):
         for c in range(7):
             own0[k, c : c + 1, :] = raw[c * BLOCKS + k]
         own0[k, 7:8, :] = jnp.zeros((1, NODES), F32)
+    own0[0, 7:8, 0:128] = own_list[0:1, :]
+    own0[0, 7:8, 128:256] = own_list[1:2, :]
 
     pl.semaphore_wait(barrier, len(targets))
 
@@ -588,7 +586,6 @@
 
         return wait
 
-    list_arrive = exchange(lists.at[4], lambda d: lists.at[d], list_send, list_recv)
     near_arrive = exchange(
         own0,
         lambda d: near0.at[pl.ds(d * BLOCKS, BLOCKS)],
@@ -617,7 +614,7 @@
         jnp.int32, (128, 128), 1
     )
     before_lane = jnp.where(before_lane, 1.0, 0.0).astype(BF16)
-    entry_of = lax.broadcasted_iota(jnp.int32, (128, 128), 0).astype(F32)
+    entry_of = lax.broadcasted_iota(jnp.int32, (32, 128), 0).astype(F32)
     row_of = lax.broadcasted_iota(jnp.int32, (8, 128), 0)
 
     def compact(wanted_rows, codes, rows, most_entries):
@@ -632,12 +629,13 @@
         )
         everything = jnp.sum(row_total, axis=0, keepdims=True)
         rank = jnp.where(wanted_rows > 0.5, rank, -1.0)
-        gathered = jnp.zeros((128, 128), F32)
+        gathered = jnp.zeros((32, 128), F32)
         for row in rows:
             gathered = gathered + jnp.where(
                 entry_of == rank[row : row + 1, :], codes[row : row + 1, :], 0.0
             )
-        gathered = jnp.broadcast_to(jnp.sum(gathered, axis=1, keepdims=True), (128, 128))
+        gathered = jnp.broadcast_to(jnp.sum(gathered, axis=1, keepdims=True), (32, 128))
+        gathered = jnp.concatenate([gathered, jnp.zeros((96, 128), F32)], axis=0)
         code = jnp.transpose(gathered)[0:8, :].astype(jnp.int32)
         return code, jnp.where(everything > most_entries + 0.5, 1.0, 0.0)
 
@@ -660,9 +658,8 @@
         spread = jnp.where(entry_row == entry_lane, 1.0, 0.0).astype(BF16)
         return dot_bf16(targets_rows.astype(F32).astype(BF16), spread, False).astype(jnp.int32)
 
-    own_ids = lists[4]
-    own_left = jnp.broadcast_to(own_ids[0:1, :], (8, 128)) - 4.0 * BLOCKS
-    own_right = jnp.broadcast_to(own_ids[1:2, :], (8, 128)) - 4.0 * BLOCKS
+    own_left = jnp.broadcast_to(own_list[0:1, :], (8, 128)) - 4.0 * BLOCKS
+    own_right = jnp.broadcast_to(own_list[1:2, :], (8, 128)) - 4.0 * BLOCKS
     inside = (own_left > -0.5) & (own_left < BLOCKS - 0.5) & (own_right > -0.5) & (own_right < BLOCKS - 0.5)
     code, overflow = compact(
         jnp.where(inside & (row_of == 0), 1.0, 0.0), own_left * 128.0 + own_right + 1.0, (0,), INNER
@@ -764,7 +761,7 @@
     slot_out[16 * INNER : INNER_WIDTH, :] = jnp.zeros((INNER_WIDTH - 16 * INNER, NODES), F32)
     evaluate_and_multiply(evaluate_inner, product_inner, 0, INNER_FOURS)
     for at in range(8):
-        list_arrive(at)
+        near_arrive(at)
     evaluate_inner(INNER - 1, tiles_of[0], INNER_FOURS)
     last_four(product_inner, 0, INNER_FOURS)
 
@@ -774,7 +771,9 @@
     add_narrow = device_row - (add_wide + 1) * 3 - 1
 
     def here(row):
-        ids = jnp.concatenate([lists[d, row : row + 1, :] for d in range(9)] + [dead_rows], axis=0)
+        lanes = slice(128 * row, 128 * row + 128)
+        rows = [own0[0, 7:8, lanes] if d == 4 else near0[d * BLOCKS, 7:8, lanes] for d in range(9)]
+        ids = jnp.concatenate(rows + [dead_rows], axis=0)
         ids = ids.astype(jnp.int32)
         is_live = ids < 200
         ids = jnp.where(is_live, ids, 0)
@@ -817,7 +816,6 @@
     inner_image = added(0, INNER_WIDTH)
 
     def prepare_next(at, carry):
-        near_arrive(at)
         for k in range(BLOCKS):
             j = (at + at // 4) * BLOCKS + k
             put_pieces(pieces, j, 0, near0[j])
@@ -1059,15 +1057,12 @@
                 pltpu.VMEM((2 * BLOCKS, 1, NODES), F32),
                 pltpu.VMEM((2, SLOTS), jnp.int32),
                 pltpu.VMEM((BLOCKS, 3, NODES, 128), F32),
-                pltpu.VMEM((9, 8, 128), F32),
                 pltpu.VMEM((8, 128), jnp.int32),
                 pltpu.VMEM((8, 128), jnp.int32),
                 pltpu.SMEM((8, 128), jnp.int32),
                 pltpu.SMEM((8, 128), jnp.int32),
                 dma((5,)),
                 dma((2,)),
-                dma((8,)),
-                dma((8,)),
                 dma((8,)),
                 dma((8,)),
                 dma((ITERS - 1, 8)),

time: 67.6 us -> 67.3 us (level)
  no operation moved by 1% of the time
where the time goes in v2:
time: 67.3 us; the launch traced here: 67 us
  Pallas kernels  65 us (97%)
  between operations  2.04 us (3%)
    pallas_call x1, Pallas kernels, on_device(): *outs, flags, pairs = fast(*arguments)  64.3 us

profile of v2, /device:TPU:1, one launch (start us, length us, event | category | flops | bytes accessed | tf_op | source)
XLA Modules:
  0.0 67.0 jit_solution(65731922534980380)
XLA Ops:
  1.3 0.0 copy-start
  1.3 0.0 copy-start.1
  1.3 0.0 copy-start.2
  1.3 0.0 copy-start.3
  1.3 64.3 %shard_map.85 = (f32[18,1,256]{2,1,0:T(1,128)S(1)}, f32[18,1,256]{2,1,0:T(1,128)S(1)}, f32[18,1,256]{2,1,0:T(1,128)S(1)}, f32[1,1]{1,0:T(1,128)}, s32[2,61]{1,0:T(2,128)S(1)}) custom-call(f32[27,1,256]{2,1,0:T(1,128)} %bitcast.15, f32[18,1,256]{2,1,0:T(1,128)} %bitcast.17, f32[18,1,256]{2,1,0:T(1,128)} %bitcast.19, f32[18,1,256]{2,1,0:T(1,128)} %bitcast.21, ...), custom_call_target="tpu_custom_call" | custom-call | flops 212336640 | bytes 200000 | tf_op jit(solution)/shard_map/pallas_call | solution.py:1136
  66.3 0.0 copy-done
  66.4 0.0 copy-done.1
  66.4 0.0 copy-done.2
  66.4 0.0 copy-done.3
  66.4 0.6 shard_map.86
  (1 shorter events, 0.0 us)
Async XLA Ops:
  1.3 65.1 %copy-start = (f32[3,1,1,9,256]{4,2,3,1,0:T(1,128)S(1)}, f32[3,1,1,9,256]{4,2,3,1,0:T(1,128)}, u32[]{:S(2)}) copy-start(f32[3,1,1,9,256]{4,2,3,1,0:T(1,128)} %param.8) | copy-start | bytes 82948
  1.3 65.1 %copy-start.1 = (f32[2,1,1,9,256]{4,2,3,1,0:T(1,128)S(1)}, f32[2,1,1,9,256]{4,2,3,1,0:T(1,128)}, u32[]{:S(2)}) copy-start(f32[2,1,1,9,256]{4,2,3,1,0:T(1,128)} %param.9) | copy-start | bytes 55300
  1.3 65.1 %copy-start.2 = (f32[2,1,1,9,256]{4,2,3,1,0:T(1,128)S(1)}, f32[2,1,1,9,256]{4,2,3,1,0:T(1,128)}, u32[]{:S(2)}) copy-start(f32[2,1,1,9,256]{4,2,3,1,0:T(1,128)} %param.10) | copy-start | bytes 55300
  1.3 65.1 %copy-start.3 = (f32[2,1,1,9,256]{4,2,3,1,0:T(1,128)S(1)}, f32[2,1,1,9,256]{4,2,3,1,0:T(1,128)}, u32[]{:S(2)}) copy-start(f32[2,1,1,9,256]{4,2,3,1,0:T(1,128)} %param.11) | copy-start | bytes 55300

commit v3 on v2

--- a/solution.py
+++ b/solution.py
@@ -462,9 +462,25 @@
 P_ROWS = 24
 
 
+MOST = 31
+
+
+def two_stage_peers(wide, narrow, narrow_size):
+    x, rank = wide // 16, wide % 16
+    first = [
+        ((wide - rank + (rank + step) % 16, narrow), min(step, 16 - step)) for step in range(1, 16)
+    ]
+    second = []
+    for right in range(4):
+        for up in range(narrow_size):
+            if right or up:
+                device = (rank + (x + right) % 4 * 16, (narrow + up) % narrow_size)
+                second.append((device, min(right, 4 - right) + min(up, narrow_size - up)))
+    return first, second
+
+
 def fast_body(
     sizes,
-    stages,
     coord_ref,
     sol_ref,
     res_ref,
@@ -521,7 +537,7 @@
             to_wide = (wide + (d // 3 - 1) + wide_size) % wide_size
             to_narrow = (narrow + (d % 3 - 1) + narrow_size) % narrow_size
             neighbours.append((d, (to_wide, to_narrow)))
-    peers = stage_peers(wide, narrow, stages)
+    peers = two_stage_peers(wide, narrow, narrow_size)
 
     loads = [
         pltpu.make_async_copy(source, landing, load_sems.at[at])
@@ -539,7 +555,7 @@
         load.start()
 
     barrier = pltpu.get_barrier_semaphore()
-    targets = [device for _, device in neighbours] + [device for group in peers for device in group]
+    targets = [device for _, device in neighbours] + [device for group in peers for device, _ in group]
     for device in targets:
         pl.semaphore_signal(barrier, inc=1, device_id=device, device_id_type=MESH)
 
@@ -913,14 +929,13 @@
     for stage, group_peers in enumerate(peers):
         sums[stage] = gram
         copies = []
-        count = len(group_peers)
-        for at in sorted(range(count), key=lambda at: -min(at + 1, count - at)):
+        for at in sorted(range(len(group_peers)), key=lambda at: -group_peers[at][1]):
             copy = pltpu.make_async_remote_copy(
                 src_ref=sums.at[stage],
                 dst_ref=sum_in.at[stage, at],
                 send_sem=sum_send.at[stage, at],
                 recv_sem=sum_recv.at[stage, at],
-                device_id=group_peers[at],
+                device_id=group_peers[at][0],
                 device_id_type=MESH,
             )
             copy.start()
@@ -1036,7 +1051,7 @@
         anywhere = pl.BlockSpec(memory_space=pl.ANY)
         dma = pltpu.SemaphoreType.DMA
         fast = pl.pallas_call(
-            functools.partial(fast_body, sizes, stages),
+            functools.partial(fast_body, sizes),
             out_shape=(fields, fields, fields, jax.ShapeDtypeStruct((1, 1), F32), jax.ShapeDtypeStruct((2, SLOTS), jnp.int32)),
             in_specs=[anywhere] * 5 + [vmem],
             out_specs=(vmem, vmem, vmem, pl.BlockSpec(memory_space=pltpu.SMEM), vmem),
@@ -1051,8 +1066,8 @@
                 pltpu.VMEM((FAST_WIDTH, NODES), F32),
                 pltpu.VMEM((FAST_TABLE, FAST_WIDTH), BF16),
                 pltpu.VMEM((ITERS + 1, 2, ROWS, 128), F32),
-                pltpu.VMEM((len(stages), 8, 128), F32),
-                pltpu.VMEM((len(stages), most, 8, 128), F32),
+                pltpu.VMEM((2, 8, 128), F32),
+                pltpu.VMEM((2, MOST, 8, 128), F32),
                 pltpu.VMEM((7 * BLOCKS, 1, NODES), F32),
                 pltpu.VMEM((2 * BLOCKS, 1, NODES), F32),
                 pltpu.VMEM((2, SLOTS), jnp.int32),
@@ -1067,8 +1082,8 @@
                 dma((8,)),
                 dma((ITERS - 1, 8)),
                 dma((ITERS - 1, 8)),
-                dma((len(stages), most)),
-                dma((len(stages), most)),
+                dma((2, MOST)),
+                dma((2, MOST)),
             ],
             compiler_params=pltpu.CompilerParams(
                 collective_id=0, has_side_effects=True, vmem_limit_bytes=60 * 1024 * 1024

time: 67.3 us -> 66.1 us (0.982)
  Pallas kernels: 65 us -> 63.8 us
    pallas_call x1, Pallas kernels: 64.3 us -> 63.1 us  [on_device(): *outs, flags, pairs = fast(*arguments)]
where the time goes in v3:
time: 66.1 us; the launch traced here: 65.8 us
  Pallas kernels  63.8 us (97%)
  between operations  2.04 us (3%)
    pallas_call x1, Pallas kernels, on_device(): *outs, flags, pairs = fast(*arguments)  63.1 us

profile of v3, /device:TPU:1, one launch (start us, length us, event | category | flops | bytes accessed | tf_op | source)
XLA Modules:
  0.0 65.8 jit_solution(4455244103254978552)
XLA Ops:
  1.3 0.0 copy-start
  1.3 0.0 copy-start.1
  1.3 0.0 copy-start.2
  1.3 0.0 copy-start.3
  1.3 63.1 %shard_map.85 = (f32[18,1,256]{2,1,0:T(1,128)S(1)}, f32[18,1,256]{2,1,0:T(1,128)S(1)}, f32[18,1,256]{2,1,0:T(1,128)S(1)}, f32[1,1]{1,0:T(1,128)}, s32[2,61]{1,0:T(2,128)S(1)}) custom-call(f32[27,1,256]{2,1,0:T(1,128)} %bitcast.15, f32[18,1,256]{2,1,0:T(1,128)} %bitcast.17, f32[18,1,256]{2,1,0:T(1,128)} %bitcast.19, f32[18,1,256]{2,1,0:T(1,128)} %bitcast.21, ...), custom_call_target="tpu_custom_call" | custom-call | flops 212336640 | bytes 200000 | tf_op jit(solution)/shard_map/pallas_call | solution.py:1151
  65.1 0.0 copy-done
  65.2 0.0 copy-done.1
  65.2 0.0 copy-done.2
  65.2 0.0 copy-done.3
  65.2 0.6 shard_map.86
  (1 shorter events, 0.0 us)
Async XLA Ops:
  1.3 63.9 %copy-start = (f32[3,1,1,9,256]{4,2,3,1,0:T(1,128)S(1)}, f32[3,1,1,9,256]{4,2,3,1,0:T(1,128)}, u32[]{:S(2)}) copy-start(f32[3,1,1,9,256]{4,2,3,1,0:T(1,128)} %param.8) | copy-start | bytes 82948
  1.3 63.9 %copy-start.1 = (f32[2,1,1,9,256]{4,2,3,1,0:T(1,128)S(1)}, f32[2,1,1,9,256]{4,2,3,1,0:T(1,128)}, u32[]{:S(2)}) copy-start(f32[2,1,1,9,256]{4,2,3,1,0:T(1,128)} %param.9) | copy-start | bytes 55300
  1.3 63.9 %copy-start.2 = (f32[2,1,1,9,256]{4,2,3,1,0:T(1,128)S(1)}, f32[2,1,1,9,256]{4,2,3,1,0:T(1,128)}, u32[]{:S(2)}) copy-start(f32[2,1,1,9,256]{4,2,3,1,0:T(1,128)} %param.10) | copy-start | bytes 55300
  1.3 63.9 %copy-start.3 = (f32[2,1,1,9,256]{4,2,3,1,0:T(1,128)S(1)}, f32[2,1,1,9,256]{4,2,3,1,0:T(1,128)}, u32[]{:S(2)}) copy-start(f32[2,1,1,9,256]{4,2,3,1,0:T(1,128)} %param.11) | copy-start | bytes 55300

commit v4 on v3

--- a/solution.py
+++ b/solution.py
@@ -707,15 +707,14 @@
     def evaluate(block, other, refs, at):
         high_ref, low_ref = refs
         block = jnp.clip(block, 0, BLOCKS - 1)
-        for h in range(2):
-            lanes = slice(128 * h, 128 * h + 128)
-            others = [
-                jnp.broadcast_to(other[4 + axis : 5 + axis, lanes], (CHUNK, 128)) for axis in range(3)
-            ]
-            for first in range(0, NODES, CHUNK):
+        others = [jnp.broadcast_to(other[4 + axis : 5 + axis, :], (CHUNK, NODES)) for axis in range(3)]
+        for first in range(0, NODES, CHUNK):
+            columns = [own_columns[block, axis, first : first + CHUNK, :] for axis in range(3)]
+            for h in range(2):
+                lanes = slice(128 * h, 128 * h + 128)
                 squared = None
                 for axis in range(3):
-                    offset = own_columns[block, axis, first : first + CHUNK, :] - others[axis]
+                    offset = columns[axis] - others[axis][:, lanes]
                     squared = offset * offset if squared is None else squared + offset * offset
                 squared = jnp.minimum(squared, RADIUS * RADIUS)
                 distance = squared * lax.rsqrt(jnp.maximum(squared, 1e-36))

time: 66.1 us -> 66.2 us (level)
  no operation moved by 1% of the time
where the time goes in v4:
time: 66.2 us; the launch traced here: 66 us
  Pallas kernels  63.9 us (97%)
  between operations  2.04 us (3%)
    pallas_call x1, Pallas kernels, on_device(): *outs, flags, pairs = fast(*arguments)  63.3 us

profile of v4, /device:TPU:1, one launch (start us, length us, event | category | flops | bytes accessed | tf_op | source)
XLA Modules:
  0.0 66.0 jit_solution(8870964750804722368)
XLA Ops:
  1.3 0.0 copy-start
  1.3 0.0 copy-start.1
  1.3 0.0 copy-start.2
  1.3 0.0 copy-start.3
  1.3 63.3 %shard_map.85 = (f32[18,1,256]{2,1,0:T(1,128)S(1)}, f32[18,1,256]{2,1,0:T(1,128)S(1)}, f32[18,1,256]{2,1,0:T(1,128)S(1)}, f32[1,1]{1,0:T(1,128)}, s32[2,61]{1,0:T(2,128)S(1)}) custom-call(f32[27,1,256]{2,1,0:T(1,128)} %bitcast.15, f32[18,1,256]{2,1,0:T(1,128)} %bitcast.17, f32[18,1,256]{2,1,0:T(1,128)} %bitcast.19, f32[18,1,256]{2,1,0:T(1,128)} %bitcast.21, ...), custom_call_target="tpu_custom_call" | custom-call | flops 212336640 | bytes 200000 | tf_op jit(solution)/shard_map/pallas_call | solution.py:1150
  65.3 0.0 copy-done
  65.3 0.0 copy-done.1
  65.3 0.0 copy-done.2
  65.3 0.0 copy-done.3
  65.3 0.6 shard_map.86
  (1 shorter events, 0.0 us)
Async XLA Ops:
  1.3 64.0 %copy-start = (f32[3,1,1,9,256]{4,2,3,1,0:T(1,128)S(1)}, f32[3,1,1,9,256]{4,2,3,1,0:T(1,128)}, u32[]{:S(2)}) copy-start(f32[3,1,1,9,256]{4,2,3,1,0:T(1,128)} %param.8) | copy-start | bytes 82948
  1.3 64.0 %copy-start.1 = (f32[2,1,1,9,256]{4,2,3,1,0:T(1,128)S(1)}, f32[2,1,1,9,256]{4,2,3,1,0:T(1,128)}, u32[]{:S(2)}) copy-start(f32[2,1,1,9,256]{4,2,3,1,0:T(1,128)} %param.9) | copy-start | bytes 55300
  1.3 64.0 %copy-start.2 = (f32[2,1,1,9,256]{4,2,3,1,0:T(1,128)S(1)}, f32[2,1,1,9,256]{4,2,3,1,0:T(1,128)}, u32[]{:S(2)}) copy-start(f32[2,1,1,9,256]{4,2,3,1,0:T(1,128)} %param.10) | copy-start | bytes 55300
  1.3 64.0 %copy-start.3 = (f32[2,1,1,9,256]{4,2,3,1,0:T(1,128)S(1)}, f32[2,1,1,9,256]{4,2,3,1,0:T(1,128)}, u32[]{:S(2)}) copy-start(f32[2,1,1,9,256]{4,2,3,1,0:T(1,128)} %param.11) | copy-start | bytes 55300
